TPU v7x, 32 devices: a whole 2x2x4 slice. The times are simulated.
32 devices in a mesh: parts: 2 (over y), gx: 16 (over z, x, core).
Axes of the slice: x: 2, y: 2, z: 4, core: 2. Of those that a mesh axis runs over, the one named last changes fastest.
Arguments:
- e_start: float32 [3, 256, 16, 128], P(None, ('parts', 'gx')), parts along dimension 1, may hold values from -6 to 6
- h_start: float32 [3, 256, 16, 128], P(None, ('parts', 'gx')), parts along dimension 1, may hold values from -6 to 6
- background: float32 [256, 16, 128], P(('parts', 'gx')), parts along dimension 0, may hold values from 1 to 4
- design: float32 [256, 16, 128], P(('parts', 'gx')), parts along dimension 0, may hold values from -6 to 6
- design_mask: int32 [256, 16, 128], P(('parts', 'gx')), parts along dimension 0, may hold values 0 or 1
- plane_counts: int32 [32], P(('parts', 'gx')), parts along dimension 0, may hold values from 1 to 8, 32 in all
- plane_rows: int32 [32, 8], P(('parts', 'gx')), parts along dimension 0, may hold values from 0 to 7, as said below
- source_cells: int32 [128], P('parts'), parts along dimension 0, may hold values from 0 to 262143
- source_amp: float32 [128], P('parts'), parts along dimension 0, may hold values from -8 to 8
- target: float32 [16, 128], replicated, may hold values from 0.1 to 1
Outputs:
- new_design: float32 [256, 16, 128], P(('parts', 'gx')), parts along dimension 0
- final_field: float32 [3, 256, 16, 128], P(None, ('parts', 'gx')), parts along dimension 1
- far_intensity: float32 [32, 128], P('parts'), parts along dimension 0
There are 2 independent parts, one for each index of `parts`. A program takes and returns all parts, laid end to end along the dimension named above; an argument that names none is the same for every part. Nothing has to cross between parts.
Inputs may be any that keep to these rules, and one draw needn't show every extreme that they name: Block d holds plane_counts[d] monitor planes; the counts sum to 32. `plane_rows`: each row holds 8 distinct local row numbers; slot s of block d is a monitor plane when s < plane_counts[d].
All inputs are finite; a program needn't handle non-finite values. No bound on the sum of `design_mask` on one device may be relied on, other than what follows from the above.
Results may differ from a plain program's by a relative error of at most 0.0003.
Values sent between devices are 32-bit elements; how exact they have to be, the bound alone decides.
A program may use at most 64 MiB of HBM per device.

v0:
```python
import math

import jax
import jax.numpy as jnp
from jax import lax
from jax.sharding import PartitionSpec as P

STEPS = 8
ITERS = 2
KY = 128
KZ = 16
PLANES_DEV = 2


COURANT = 0.5
OMEGA = 0.7
SPAN_EPS = 8.0
RATE = 0.5
EPSILON = 1e-06
HIGH = lax.Precision.HIGHEST


def shifted(block, axis, distance):
    devices = range(lax.axis_size(axis))
    route = [(i - distance, i) for i in devices if i - distance in devices]
    return lax.ppermute(block, axis, route)


def forward_diff(field, axis):
    length = field.shape[axis]
    edge = jnp.zeros_like(lax.slice_in_dim(field, 0, 1, axis=axis))
    return jnp.concatenate([lax.slice_in_dim(field, 1, length, axis=axis), edge], axis=axis) - field


def backward_diff(field, axis):
    length = field.shape[axis]
    edge = jnp.zeros_like(lax.slice_in_dim(field, 0, 1, axis=axis))
    return field - jnp.concatenate(
        [edge, lax.slice_in_dim(field, 0, length - 1, axis=axis)], axis=axis
    )


def update_h(electric, magnetic, after):
    curl_x = forward_diff(electric[2], 2) - forward_diff(electric[1], 1)
    curl_y = forward_diff(electric[0], 1) - (
        jnp.concatenate([electric[2][1:], after[1]], axis=0) - electric[2]
    )
    curl_z = (
        jnp.concatenate([electric[1][1:], after[0]], axis=0)
        - electric[1]
        - forward_diff(electric[0], 2)
    )
    return jnp.stack(
        [
            magnetic[0] - COURANT * curl_x,
            magnetic[1] - COURANT * curl_y,
            magnetic[2] - COURANT * curl_z,
        ]
    )


def update_e(electric, magnetic, inverse, before, drive, time_value):
    curl_x = backward_diff(magnetic[2], 2) - backward_diff(magnetic[1], 1)
    curl_y = backward_diff(magnetic[0], 1) - (
        magnetic[2] - jnp.concatenate([before[1], magnetic[2][:-1]], axis=0)
    )
    curl_z = (
        magnetic[1]
        - jnp.concatenate([before[0], magnetic[1][:-1]], axis=0)
        - backward_diff(magnetic[0], 2)
    )
    parts = [
        electric[0] + COURANT * inverse * curl_x,
        electric[1] + COURANT * inverse * curl_y,
        electric[2] + COURANT * inverse * curl_z,
    ]
    for component, kind, source in drive:
        factor = math.cos(OMEGA * time_value) if kind == "cos" else math.sin(OMEGA * time_value)
        parts[component] = parts[component] + factor * source
    return jnp.stack(parts)


def angle_tables(width_y, depth_z):
    angle = (jnp.arange(KY, dtype=jnp.float32) + 0.5) * (math.pi / (2 * KY))
    wavenumber = OMEGA / COURANT
    wave_y = wavenumber * jnp.sin(angle)
    wave_x = wavenumber * jnp.cos(angle)
    wave_z = (jnp.arange(KZ, dtype=jnp.float32) + 0.5) * (math.pi / KZ)
    phase_y = jnp.arange(width_y, dtype=jnp.float32)[:, None] * wave_y[None, :]
    cos_y = jnp.cos(phase_y)
    sin_y = jnp.sin(phase_y)
    to_far = jnp.concatenate(
        [jnp.concatenate([cos_y, -sin_y], axis=1), jnp.concatenate([sin_y, cos_y], axis=1)], axis=0
    )
    to_near = jnp.concatenate(
        [jnp.concatenate([cos_y.T, -sin_y.T], axis=1), jnp.concatenate([sin_y.T, cos_y.T], axis=1)],
        axis=0,
    )
    phase_z = jnp.arange(depth_z, dtype=jnp.float32)[:, None] * wave_z[None, :]
    return (to_far, to_near, jnp.cos(phase_z), jnp.sin(phase_z), wave_x)


def project(near_re, near_im, plane_x, tables):
    to_far, to_near, cos_z, sin_z, wave_x = tables
    stacked = jnp.concatenate([near_re, near_im], axis=-1)
    flat = jnp.dot(
        stacked.reshape(-1, stacked.shape[-1]),
        to_far,
        precision=HIGH,
        preferred_element_type=jnp.float32,
    )
    along_y = flat.reshape(stacked.shape[:-1] + (to_far.shape[1],))
    part_re = along_y[..., :KY]
    part_im = along_y[..., KY:]
    zed_re = jnp.einsum("fszk,zm->fsmk", part_re, cos_z, precision=HIGH) + jnp.einsum(
        "fszk,zm->fsmk", part_im, sin_z, precision=HIGH
    )
    zed_im = jnp.einsum("fszk,zm->fsmk", part_im, cos_z, precision=HIGH) - jnp.einsum(
        "fszk,zm->fsmk", part_re, sin_z, precision=HIGH
    )
    phase_x = plane_x[:, None] * wave_x[None, :]
    cos_x = jnp.cos(phase_x)[None, :, None, :]
    sin_x = jnp.sin(phase_x)[None, :, None, :]
    return (
        jnp.sum(cos_x * zed_re + sin_x * zed_im, axis=1),
        jnp.sum(cos_x * zed_im - sin_x * zed_re, axis=1),
    )


def back_project(weight_re, weight_im, plane_x, tables):
    to_far, to_near, cos_z, sin_z, wave_x = tables
    phase_x = plane_x[:, None] * wave_x[None, :]
    cos_x = jnp.cos(phase_x)[None, :, None, :]
    sin_x = jnp.sin(phase_x)[None, :, None, :]
    slot_re = cos_x * weight_re[:, None] + sin_x * weight_im[:, None]
    slot_im = cos_x * weight_im[:, None] - sin_x * weight_re[:, None]
    zed_re = jnp.einsum("fsmk,zm->fszk", slot_re, cos_z, precision=HIGH) + jnp.einsum(
        "fsmk,zm->fszk", slot_im, sin_z, precision=HIGH
    )
    zed_im = jnp.einsum("fsmk,zm->fszk", slot_im, cos_z, precision=HIGH) - jnp.einsum(
        "fsmk,zm->fszk", slot_re, sin_z, precision=HIGH
    )
    stacked = jnp.concatenate([zed_re, zed_im], axis=-1)
    flat = jnp.dot(
        stacked.reshape(-1, stacked.shape[-1]),
        to_near,
        precision=HIGH,
        preferred_element_type=jnp.float32,
    )
    near = flat.reshape(stacked.shape[:-1] + (to_near.shape[1],))
    half = to_near.shape[1] // 2
    return (near[..., :half], near[..., half:])


def place_sources(source_cells, source_amp, first_row, row_count, depth_z, width_y):
    cells = row_count * depth_z * width_y
    local_ids = source_cells - first_row * depth_z * width_y
    inside = (local_ids >= 0) & (local_ids < cells)
    flat = (
        jnp.zeros((cells,), jnp.float32)
        .at[jnp.where(inside, local_ids, 0)]
        .add(jnp.where(inside, source_amp, 0.0))
    )
    return flat.reshape(row_count, depth_z, width_y)


def scaled_back(weight_re, weight_im, rows_here, valid_here, first_row, tables, near_scale):
    plane_here = (first_row + rows_here).astype(jnp.float32)
    back_re, back_im = back_project(weight_re, weight_im, plane_here, tables)
    valid_four = valid_here[None, :, None, None]
    return (back_re * near_scale * valid_four, back_im * near_scale * valid_four)


def body(
    e_start,
    h_start,
    background,
    design,
    design_mask,
    plane_counts,
    plane_rows,
    source_cells,
    source_amp,
    target,
):
    rows_dev, depth_z, width_y = background.shape
    devices = lax.axis_size("gx")
    index = lax.axis_index("gx")
    slots = plane_rows.shape[1]
    slot_rows = plane_rows[0]
    slot_valid = (jnp.arange(slots, dtype=jnp.int32) < plane_counts[0]).astype(jnp.float32)
    valid_four = slot_valid[None, :, None, None]
    plane_x = (index * rows_dev + slot_rows).astype(jnp.float32)
    mask_float = design_mask.astype(jnp.float32)
    tables = angle_tables(width_y, depth_z)
    far_scale = 1.0 / math.sqrt(width_y * depth_z * PLANES_DEV * devices * STEPS)
    near_scale = 1.0 / math.sqrt(KY * KZ)
    grid_cells = rows_dev * devices * depth_z * width_y
    source_field = place_sources(
        source_cells, source_amp, index * rows_dev, rows_dev, depth_z, width_y
    )

    def march(electric, magnetic, inverse, drive, times, record, carry):
        for time_value in times:
            after = shifted(electric[1:3, :1], "gx", -1)
            magnetic = update_h(electric, magnetic, after)
            before = shifted(magnetic[1:3, -1:], "gx", 1)
            electric = update_e(electric, magnetic, inverse, before, drive, time_value)
            carry = record(carry, electric, magnetic, time_value)
        return (electric, carry)

    current = design
    final_field = e_start
    intensity = jnp.zeros((KZ, KY), jnp.float32)
    for iteration in range(ITERS):
        squash = jax.nn.sigmoid(current)
        inverse = 1.0 / (background + SPAN_EPS * mask_float * squash)
        forward_drive = [(2, "sin", source_field)]

        def record_forward(carry, electric, magnetic, time_value):
            history, monitor_re, monitor_im = carry
            plane = jnp.stack(
                [
                    jnp.take(electric[1], slot_rows, axis=0)
                    + jnp.take(magnetic[2], slot_rows, axis=0),
                    jnp.take(electric[2], slot_rows, axis=0)
                    - jnp.take(magnetic[1], slot_rows, axis=0),
                ]
            )
            return (
                history + [electric],
                monitor_re + math.cos(OMEGA * time_value) * plane,
                monitor_im - math.sin(OMEGA * time_value) * plane,
            )

        empty = jnp.zeros((2, slots, depth_z, width_y), jnp.float32)
        final_field, forward_state = march(
            e_start,
            h_start,
            inverse,
            forward_drive,
            list(range(1, STEPS + 1)),
            record_forward,
            ([], empty, empty),
        )
        history, monitor_re, monitor_im = forward_state
        far_re, far_im = project(monitor_re * valid_four, monitor_im * valid_four, plane_x, tables)
        far_re = far_re * far_scale
        far_im = far_im * far_scale
        total_re, total_im = lax.psum((far_re, far_im), "gx")
        weight_re = 2.0 * target * total_re
        weight_im = -2.0 * target * total_im
        intensity = jnp.sum(total_re * total_re + total_im * total_im, axis=0)
        back_re, back_im = scaled_back(
            weight_re, weight_im, slot_rows, slot_valid, index * rows_dev, tables, near_scale
        )
        dense = (
            jnp.zeros((2, 2, rows_dev, depth_z, width_y), jnp.float32)
            .at[:, :, slot_rows]
            .add(jnp.stack([back_re, back_im], axis=1))
        )
        sources = dense.reshape((4, rows_dev, depth_z, width_y))
        back_drive = [
            (1, "cos", sources[0]),
            (1, "sin", sources[1]),
            (2, "cos", sources[2]),
            (2, "sin", sources[3]),
        ]

        def record_adjoint(carry, electric, magnetic, time_value):
            return carry + jnp.sum(history[time_value - 1] * electric, axis=0)

        zero_field = jnp.zeros_like(e_start)
        unused_field, sensitivity = march(
            zero_field,
            zero_field,
            inverse,
            back_drive,
            [STEPS - count for count in range(STEPS)],
            record_adjoint,
            jnp.zeros_like(background),
        )
        gradient = sensitivity * mask_float * SPAN_EPS * squash * (1.0 - squash)
        total = lax.psum(jnp.sum(gradient * gradient), "gx")
        current = current + RATE * gradient / jnp.sqrt(total / grid_cells + EPSILON)
    return (current, final_field, intensity)


def solution(mesh):
    return jax.shard_map(
        body,
        mesh=mesh,
        in_specs=(
            P(None, ("parts", "gx"), None, None),
            P(None, ("parts", "gx"), None, None),
            P(("parts", "gx"), None, None),
            P(("parts", "gx"), None, None),
            P(("parts", "gx"), None, None),
            P(("parts", "gx")),
            P(("parts", "gx"), None),
            P("parts"),
            P("parts"),
            P(),
        ),
        out_specs=(
            P(("parts", "gx"), None, None),
            P(None, ("parts", "gx"), None, None),
            P("parts", None),
        ),
        check_vma=False,
    )
```

profile of v0, /device:TPU:0, one launch (start us, length us, event | category | flops | bytes accessed | tf_op | source)
XLA Modules:
  0.0 530.3 jit_solution(15221701461730103651)
XLA Ops:
  8.6 3.7 collective-permute-start.1
  16.8 2.4 collective-permute-done.2
  19.2 4.6 collective-permute-start.3
  28.0 6.2 %collective-permute-start.5 = (f32[2,1,16,128]{3,2,1,0:T(8,128)S(1)}, f32[2,1,16,128]{3,2,1,0:T(8,128)S(1)}, u32[]{:S(2)}, u32[]{:S(2)}) collective-permute-start(f32[2,1,16,128]{3,2,1,0:T(8,128)S(1)} %pad_maximum_fusion.70), channel_id=1, source_target_pairs={{0,1},{1,2},{2,3},{3,4},{4,5},{5,6},{6,7},{7,8},{8,9},{9,10},{10,1... | collective-permute-start | bytes 49160 | tf_op jit(solution)/shard_map/ppermute | solution.py:26
  38.3 5.5 %collective-permute-start.7 = (f32[2,1,16,128]{3,2,1,0:T(8,128)S(1)}, f32[2,1,16,128]{3,2,1,0:T(8,128)S(1)}, u32[]{:S(2)}, u32[]{:S(2)}) collective-permute-start(f32[2,1,16,128]{3,2,1,0:T(8,128)S(1)} %pad_maximum_fusion.68), channel_id=1, source_target_pairs={{0,1},{1,2},{2,3},{3,4},{4,5},{5,6},{6,7},{7,8},{8,9},{9,10},{10,1... | collective-permute-start | bytes 49160 | tf_op jit(solution)/shard_map/ppermute | solution.py:26
  47.8 5.4 %collective-permute-start.9 = (f32[2,1,16,128]{3,2,1,0:T(8,128)S(1)}, f32[2,1,16,128]{3,2,1,0:T(8,128)S(1)}, u32[]{:S(2)}, u32[]{:S(2)}) collective-permute-start(f32[2,1,16,128]{3,2,1,0:T(8,128)S(1)} %pad_maximum_fusion.66), channel_id=1, source_target_pairs={{0,1},{1,2},{2,3},{3,4},{4,5},{5,6},{6,7},{7,8},{8,9},{9,10},{10,1... | collective-permute-start | bytes 49160 | tf_op jit(solution)/shard_map/ppermute | solution.py:26
  57.3 5.4 %collective-permute-start.11 = (f32[2,1,16,128]{3,2,1,0:T(8,128)S(1)}, f32[2,1,16,128]{3,2,1,0:T(8,128)S(1)}, u32[]{:S(2)}, u32[]{:S(2)}) collective-permute-start(f32[2,1,16,128]{3,2,1,0:T(8,128)S(1)} %pad_maximum_fusion.64), channel_id=1, source_target_pairs={{0,1},{1,2},{2,3},{3,4},{4,5},{5,6},{6,7},{7,8},{8,9},{9,10},{10,1... | collective-permute-start | bytes 49160 | tf_op jit(solution)/shard_map/ppermute | solution.py:26
  66.8 5.4 %collective-permute-start.13 = (f32[2,1,16,128]{3,2,1,0:T(8,128)S(1)}, f32[2,1,16,128]{3,2,1,0:T(8,128)S(1)}, u32[]{:S(2)}, u32[]{:S(2)}) collective-permute-start(f32[2,1,16,128]{3,2,1,0:T(8,128)S(1)} %pad_maximum_fusion.62), channel_id=1, source_target_pairs={{0,1},{1,2},{2,3},{3,4},{4,5},{5,6},{6,7},{7,8},{8,9},{9,10},{10,1... | collective-permute-start | bytes 49160 | tf_op jit(solution)/shard_map/ppermute | solution.py:26
  102.2 5.9 %collective-permute-start.15 = (f32[2,1,16,128]{3,2,1,0:T(8,128)S(1)}, f32[2,1,16,128]{3,2,1,0:T(8,128)S(1)}, u32[]{:S(2)}, u32[]{:S(2)}) collective-permute-start(f32[2,1,16,128]{3,2,1,0:T(8,128)S(1)} %pad_maximum_fusion.60), channel_id=1, source_target_pairs={{0,1},{1,2},{2,3},{3,4},{4,5},{5,6},{6,7},{7,8},{8,9},{9,10},{10,1... | collective-permute-start | bytes 49160 | tf_op jit(solution)/shard_map/ppermute | solution.py:26
  130.8 59.3 %all-reduce.237 = (f32[2,16,128]{2,1,0:T(8,128)S(1)}, f32[2,16,128]{2,1,0:T(8,128)S(1)}) all-reduce(f32[2,16,128]{2,1,0:T(8,128)S(1)} %multiply_bitcast_fusion.2, f32[2,16,128]{2,1,0:T(8,128)S(1)} %multiply_bitcast_fusion.3), channel_id=1, replica_groups=mesh['parts'=2,'gx'=16] {'gx'}, use_global_device_ids=true, to_apply=%region_4.6 | all-reduce | flops 8192 | bytes 65536 | tf_op jit(solution)/shard_map/psum | solution.py:250
  203.7 4.5 collective-permute-start.21
  212.3 4.5 collective-permute-start.23
  221.0 4.5 collective-permute-start.25
  229.6 4.5 collective-permute-start.27
  238.3 4.8 collective-permute-start.29
  247.2 5.6 %collective-permute-start.31 = (f32[2,1,16,128]{3,2,1,0:T(8,128)S(1)}, f32[2,1,16,128]{3,2,1,0:T(8,128)S(1)}, u32[]{:S(2)}, u32[]{:S(2)}) collective-permute-start(f32[2,1,16,128]{3,2,1,0:T(8,128)S(1)} %pad_maximum_fusion.45), channel_id=1, source_target_pairs={{0,1},{1,2},{2,3},{3,4},{4,5},{5,6},{6,7},{7,8},{8,9},{9,10},{10,1... | collective-permute-start | bytes 49160 | tf_op jit(solution)/shard_map/ppermute | solution.py:26
  255.2 30.4 %psum.44 = f32[]{:T(128)} all-reduce(f32[]{:T(128)} %get-tuple-element.19), channel_id=1, replica_groups=mesh['parts'=2,'gx'=16] {'gx'}, use_global_device_ids=true, to_apply=%region_15.17 | all-reduce | flops 1 | bytes 8 | tf_op jit(solution)/shard_map/psum | solution.py:284
  290.5 3.4 collective-permute-start.33
  298.0 4.5 collective-permute-start.35
  306.6 4.5 collective-permute-start.37
  315.2 4.5 collective-permute-start.39
  323.8 4.6 collective-permute-start.41
  332.6 5.4 %collective-permute-start.43 = (f32[2,1,16,128]{3,2,1,0:T(8,128)S(1)}, f32[2,1,16,128]{3,2,1,0:T(8,128)S(1)}, u32[]{:S(2)}, u32[]{:S(2)}) collective-permute-start(f32[2,1,16,128]{3,2,1,0:T(8,128)S(1)} %pad_maximum_fusion.33), channel_id=1, source_target_pairs={{0,1},{1,2},{2,3},{3,4},{4,5},{5,6},{6,7},{7,8},{8,9},{9,10},{10,1... | collective-permute-start | bytes 49160 | tf_op jit(solution)/shard_map/ppermute | solution.py:26
  342.1 5.4 %collective-permute-start.45 = (f32[2,1,16,128]{3,2,1,0:T(8,128)S(1)}, f32[2,1,16,128]{3,2,1,0:T(8,128)S(1)}, u32[]{:S(2)}, u32[]{:S(2)}) collective-permute-start(f32[2,1,16,128]{3,2,1,0:T(8,128)S(1)} %pad_maximum_fusion.31), channel_id=1, source_target_pairs={{0,1},{1,2},{2,3},{3,4},{4,5},{5,6},{6,7},{7,8},{8,9},{9,10},{10,1... | collective-permute-start | bytes 49160 | tf_op jit(solution)/shard_map/ppermute | solution.py:26
  377.1 57.6 %all-reduce.236 = (f32[2,16,128]{2,1,0:T(8,128)S(1)}, f32[2,16,128]{2,1,0:T(8,128)S(1)}) all-reduce(f32[2,16,128]{2,1,0:T(8,128)S(1)} %multiply_bitcast_fusion, f32[2,16,128]{2,1,0:T(8,128)S(1)} %multiply_bitcast_fusion.1), channel_id=1, replica_groups=mesh['parts'=2,'gx'=16] {'gx'}, use_global_device_ids=true, to_apply=%region_19.21 | all-reduce | flops 8192 | bytes 65536 | tf_op jit(solution)/shard_map/psum | solution.py:250
  448.2 4.5 collective-permute-start.49
  456.8 4.5 collective-permute-start.51
  465.4 4.5 collective-permute-start.53
  474.0 4.5 collective-permute-start.55
  482.6 4.8 collective-permute-start.57
  491.5 5.4 %collective-permute-start.59 = (f32[2,1,16,128]{3,2,1,0:T(8,128)S(1)}, f32[2,1,16,128]{3,2,1,0:T(8,128)S(1)}, u32[]{:S(2)}, u32[]{:S(2)}) collective-permute-start(f32[2,1,16,128]{3,2,1,0:T(8,128)S(1)} %pad_maximum_fusion.17), channel_id=1, source_target_pairs={{0,1},{1,2},{2,3},{3,4},{4,5},{5,6},{6,7},{7,8},{8,9},{9,10},{10,1... | collective-permute-start | bytes 49160 | tf_op jit(solution)/shard_map/ppermute | solution.py:26
  498.5 30.4 %psum.47 = f32[]{:T(128)} all-reduce(f32[]{:T(128)} %get-tuple-element.12), channel_id=1, replica_groups=mesh['parts'=2,'gx'=16] {'gx'}, use_global_device_ids=true, to_apply=%region_30.32 | all-reduce | flops 1 | bytes 8 | tf_op jit(solution)/shard_map/psum | solution.py:284
  (840 shorter events, 212.5 us)
Async XLA Ops:
  0.6 11.6 %collective-permute-start.16 = (f32[2,1,16,128]{3,2,1,0:T(8,128)S(1)}, f32[2,1,16,128]{3,2,1,0:T(8,128)S(1)}, u32[]{:S(2)}, u32[]{:S(2)}) collective-permute-start(f32[2,1,16,128]{3,2,1,0:T(8,128)S(1)} %broadcast.970), channel_id=1, source_target_pairs={{1,0},{2,1},{3,2},{4,3},{5,4},{6,5},{7,6},{8,7},{9,8},{10,9},{11,1... | collective-permute-start | bytes 49160 | tf_op jit(solution)/shard_map/ppermute | solution.py:26
  2.7 5.0 collective-permute-start
  8.6 4.7 collective-permute-start.1
  14.0 5.1 collective-permute-start.2
  19.2 5.4 %collective-permute-start.3 = (f32[2,1,16,128]{3,2,1,0:T(8,128)S(1)}, f32[2,1,16,128]{3,2,1,0:T(8,128)S(1)}, u32[]{:S(2)}, u32[]{:S(2)}) collective-permute-start(f32[2,1,16,128]{3,2,1,0:T(8,128)S(1)} %pad_maximum_fusion.72), channel_id=1, source_target_pairs={{0,1},{1,2},{2,3},{3,4},{4,5},{5,6},{6,7},{7,8},{8,9},{9,10},{10,1... | collective-permute-start | bytes 49160 | tf_op jit(solution)/shard_map/ppermute | solution.py:26
  28.0 7.0 %collective-permute-start.5 = (f32[2,1,16,128]{3,2,1,0:T(8,128)S(1)}, f32[2,1,16,128]{3,2,1,0:T(8,128)S(1)}, u32[]{:S(2)}, u32[]{:S(2)}) collective-permute-start(f32[2,1,16,128]{3,2,1,0:T(8,128)S(1)} %pad_maximum_fusion.70), channel_id=1, source_target_pairs={{0,1},{1,2},{2,3},{3,4},{4,5},{5,6},{6,7},{7,8},{8,9},{9,10},{10,1... | collective-permute-start | bytes 49160 | tf_op jit(solution)/shard_map/ppermute | solution.py:26
  38.3 6.3 %collective-permute-start.7 = (f32[2,1,16,128]{3,2,1,0:T(8,128)S(1)}, f32[2,1,16,128]{3,2,1,0:T(8,128)S(1)}, u32[]{:S(2)}, u32[]{:S(2)}) collective-permute-start(f32[2,1,16,128]{3,2,1,0:T(8,128)S(1)} %pad_maximum_fusion.68), channel_id=1, source_target_pairs={{0,1},{1,2},{2,3},{3,4},{4,5},{5,6},{6,7},{7,8},{8,9},{9,10},{10,1... | collective-permute-start | bytes 49160 | tf_op jit(solution)/shard_map/ppermute | solution.py:26
  47.8 6.2 %collective-permute-start.9 = (f32[2,1,16,128]{3,2,1,0:T(8,128)S(1)}, f32[2,1,16,128]{3,2,1,0:T(8,128)S(1)}, u32[]{:S(2)}, u32[]{:S(2)}) collective-permute-start(f32[2,1,16,128]{3,2,1,0:T(8,128)S(1)} %pad_maximum_fusion.66), channel_id=1, source_target_pairs={{0,1},{1,2},{2,3},{3,4},{4,5},{5,6},{6,7},{7,8},{8,9},{9,10},{10,1... | collective-permute-start | bytes 49160 | tf_op jit(solution)/shard_map/ppermute | solution.py:26
  57.3 6.2 %collective-permute-start.11 = (f32[2,1,16,128]{3,2,1,0:T(8,128)S(1)}, f32[2,1,16,128]{3,2,1,0:T(8,128)S(1)}, u32[]{:S(2)}, u32[]{:S(2)}) collective-permute-start(f32[2,1,16,128]{3,2,1,0:T(8,128)S(1)} %pad_maximum_fusion.64), channel_id=1, source_target_pairs={{0,1},{1,2},{2,3},{3,4},{4,5},{5,6},{6,7},{7,8},{8,9},{9,10},{10,1... | collective-permute-start | bytes 49160 | tf_op jit(solution)/shard_map/ppermute | solution.py:26
  66.8 11.0 %collective-permute-start.13 = (f32[2,1,16,128]{3,2,1,0:T(8,128)S(1)}, f32[2,1,16,128]{3,2,1,0:T(8,128)S(1)}, u32[]{:S(2)}, u32[]{:S(2)}) collective-permute-start(f32[2,1,16,128]{3,2,1,0:T(8,128)S(1)} %pad_maximum_fusion.62), channel_id=1, source_target_pairs={{0,1},{1,2},{2,3},{3,4},{4,5},{5,6},{6,7},{7,8},{8,9},{9,10},{10,1... | collective-permute-start | bytes 49160 | tf_op jit(solution)/shard_map/ppermute | solution.py:26
  75.9 4.0 collective-permute-start.17
  78.6 22.7 %collective-permute-start.14 = (f32[2,1,16,128]{3,2,1,0:T(8,128)}, f32[2,1,16,128]{3,2,1,0:T(8,128)}, u32[]{:S(2)}, u32[]{:S(2)}) collective-permute-start(f32[2,1,16,128]{3,2,1,0:T(8,128)} %pad_maximum_fusion.61), channel_id=1, source_target_pairs={{1,0},{2,1},{3,2},{4,3},{5,4},{6,5},{7,6},{8,7},{9,8},{10,9},{11,1... | collective-permute-start | bytes 49160 | tf_op jit(solution)/shard_map/ppermute | solution.py:26
  102.2 19.9 %collective-permute-start.15 = (f32[2,1,16,128]{3,2,1,0:T(8,128)S(1)}, f32[2,1,16,128]{3,2,1,0:T(8,128)S(1)}, u32[]{:S(2)}, u32[]{:S(2)}) collective-permute-start(f32[2,1,16,128]{3,2,1,0:T(8,128)S(1)} %pad_maximum_fusion.60), channel_id=1, source_target_pairs={{0,1},{1,2},{2,3},{3,4},{4,5},{5,6},{6,7},{7,8},{8,9},{9,10},{10,1... | collective-permute-start | bytes 49160 | tf_op jit(solution)/shard_map/ppermute | solution.py:26
  203.7 5.3 %collective-permute-start.21 = (f32[2,1,16,128]{3,2,1,0:T(8,128)S(1)}, f32[2,1,16,128]{3,2,1,0:T(8,128)S(1)}, u32[]{:S(2)}, u32[]{:S(2)}) collective-permute-start(f32[2,1,16,128]{3,2,1,0:T(8,128)S(1)} %pad_maximum_fusion.55), channel_id=1, source_target_pairs={{0,1},{1,2},{2,3},{3,4},{4,5},{5,6},{6,7},{7,8},{8,9},{9,10},{10,1... | collective-permute-start | bytes 49160 | tf_op jit(solution)/shard_map/ppermute | solution.py:26
  212.3 5.3 %collective-permute-start.23 = (f32[2,1,16,128]{3,2,1,0:T(8,128)S(1)}, f32[2,1,16,128]{3,2,1,0:T(8,128)S(1)}, u32[]{:S(2)}, u32[]{:S(2)}) collective-permute-start(f32[2,1,16,128]{3,2,1,0:T(8,128)S(1)} %pad_maximum_fusion.53), channel_id=1, source_target_pairs={{0,1},{1,2},{2,3},{3,4},{4,5},{5,6},{6,7},{7,8},{8,9},{9,10},{10,1... | collective-permute-start | bytes 49160 | tf_op jit(solution)/shard_map/ppermute | solution.py:26
  221.0 5.3 %collective-permute-start.25 = (f32[2,1,16,128]{3,2,1,0:T(8,128)S(1)}, f32[2,1,16,128]{3,2,1,0:T(8,128)S(1)}, u32[]{:S(2)}, u32[]{:S(2)}) collective-permute-start(f32[2,1,16,128]{3,2,1,0:T(8,128)S(1)} %pad_maximum_fusion.51), channel_id=1, source_target_pairs={{0,1},{1,2},{2,3},{3,4},{4,5},{5,6},{6,7},{7,8},{8,9},{9,10},{10,1... | collective-permute-start | bytes 49160 | tf_op jit(solution)/shard_map/ppermute | solution.py:26
  229.6 5.3 %collective-permute-start.27 = (f32[2,1,16,128]{3,2,1,0:T(8,128)S(1)}, f32[2,1,16,128]{3,2,1,0:T(8,128)S(1)}, u32[]{:S(2)}, u32[]{:S(2)}) collective-permute-start(f32[2,1,16,128]{3,2,1,0:T(8,128)S(1)} %pad_maximum_fusion.49), channel_id=1, source_target_pairs={{0,1},{1,2},{2,3},{3,4},{4,5},{5,6},{6,7},{7,8},{8,9},{9,10},{10,1... | collective-permute-start | bytes 49160 | tf_op jit(solution)/shard_map/ppermute | solution.py:26
  238.3 5.6 %collective-permute-start.29 = (f32[2,1,16,128]{3,2,1,0:T(8,128)S(1)}, f32[2,1,16,128]{3,2,1,0:T(8,128)S(1)}, u32[]{:S(2)}, u32[]{:S(2)}) collective-permute-start(f32[2,1,16,128]{3,2,1,0:T(8,128)S(1)} %pad_maximum_fusion.47), channel_id=1, source_target_pairs={{0,1},{1,2},{2,3},{3,4},{4,5},{5,6},{6,7},{7,8},{8,9},{9,10},{10,1... | collective-permute-start | bytes 49160 | tf_op jit(solution)/shard_map/ppermute | solution.py:26
  247.2 6.4 %collective-permute-start.31 = (f32[2,1,16,128]{3,2,1,0:T(8,128)S(1)}, f32[2,1,16,128]{3,2,1,0:T(8,128)S(1)}, u32[]{:S(2)}, u32[]{:S(2)}) collective-permute-start(f32[2,1,16,128]{3,2,1,0:T(8,128)S(1)} %pad_maximum_fusion.45), channel_id=1, source_target_pairs={{0,1},{1,2},{2,3},{3,4},{4,5},{5,6},{6,7},{7,8},{8,9},{9,10},{10,1... | collective-permute-start | bytes 49160 | tf_op jit(solution)/shard_map/ppermute | solution.py:26
  290.5 4.2 collective-permute-start.33
  298.0 5.3 %collective-permute-start.35 = (f32[2,1,16,128]{3,2,1,0:T(8,128)S(1)}, f32[2,1,16,128]{3,2,1,0:T(8,128)S(1)}, u32[]{:S(2)}, u32[]{:S(2)}) collective-permute-start(f32[2,1,16,128]{3,2,1,0:T(8,128)S(1)} %pad_maximum_fusion.41), channel_id=1, source_target_pairs={{0,1},{1,2},{2,3},{3,4},{4,5},{5,6},{6,7},{7,8},{8,9},{9,10},{10,1... | collective-permute-start | bytes 49160 | tf_op jit(solution)/shard_map/ppermute | solution.py:26
  306.6 5.3 %collective-permute-start.37 = (f32[2,1,16,128]{3,2,1,0:T(8,128)S(1)}, f32[2,1,16,128]{3,2,1,0:T(8,128)S(1)}, u32[]{:S(2)}, u32[]{:S(2)}) collective-permute-start(f32[2,1,16,128]{3,2,1,0:T(8,128)S(1)} %pad_maximum_fusion.39), channel_id=1, source_target_pairs={{0,1},{1,2},{2,3},{3,4},{4,5},{5,6},{6,7},{7,8},{8,9},{9,10},{10,1... | collective-permute-start | bytes 49160 | tf_op jit(solution)/shard_map/ppermute | solution.py:26
  315.2 5.3 %collective-permute-start.39 = (f32[2,1,16,128]{3,2,1,0:T(8,128)S(1)}, f32[2,1,16,128]{3,2,1,0:T(8,128)S(1)}, u32[]{:S(2)}, u32[]{:S(2)}) collective-permute-start(f32[2,1,16,128]{3,2,1,0:T(8,128)S(1)} %pad_maximum_fusion.37), channel_id=1, source_target_pairs={{0,1},{1,2},{2,3},{3,4},{4,5},{5,6},{6,7},{7,8},{8,9},{9,10},{10,1... | collective-permute-start | bytes 49160 | tf_op jit(solution)/shard_map/ppermute | solution.py:26
  323.8 5.4 %collective-permute-start.41 = (f32[2,1,16,128]{3,2,1,0:T(8,128)S(1)}, f32[2,1,16,128]{3,2,1,0:T(8,128)S(1)}, u32[]{:S(2)}, u32[]{:S(2)}) collective-permute-start(f32[2,1,16,128]{3,2,1,0:T(8,128)S(1)} %pad_maximum_fusion.35), channel_id=1, source_target_pairs={{0,1},{1,2},{2,3},{3,4},{4,5},{5,6},{6,7},{7,8},{8,9},{9,10},{10,1... | collective-permute-start | bytes 49160 | tf_op jit(solution)/shard_map/ppermute | solution.py:26
  332.6 6.2 %collective-permute-start.43 = (f32[2,1,16,128]{3,2,1,0:T(8,128)S(1)}, f32[2,1,16,128]{3,2,1,0:T(8,128)S(1)}, u32[]{:S(2)}, u32[]{:S(2)}) collective-permute-start(f32[2,1,16,128]{3,2,1,0:T(8,128)S(1)} %pad_maximum_fusion.33), channel_id=1, source_target_pairs={{0,1},{1,2},{2,3},{3,4},{4,5},{5,6},{6,7},{7,8},{8,9},{9,10},{10,1... | collective-permute-start | bytes 49160 | tf_op jit(solution)/shard_map/ppermute | solution.py:26
  342.1 28.5 %collective-permute-start.45 = (f32[2,1,16,128]{3,2,1,0:T(8,128)S(1)}, f32[2,1,16,128]{3,2,1,0:T(8,128)S(1)}, u32[]{:S(2)}, u32[]{:S(2)}) collective-permute-start(f32[2,1,16,128]{3,2,1,0:T(8,128)S(1)} %pad_maximum_fusion.31), channel_id=1, source_target_pairs={{0,1},{1,2},{2,3},{3,4},{4,5},{5,6},{6,7},{7,8},{8,9},{9,10},{10,1... | collective-permute-start | bytes 49160 | tf_op jit(solution)/shard_map/ppermute | solution.py:26
  448.2 5.3 %collective-permute-start.49 = (f32[2,1,16,128]{3,2,1,0:T(8,128)S(1)}, f32[2,1,16,128]{3,2,1,0:T(8,128)S(1)}, u32[]{:S(2)}, u32[]{:S(2)}) collective-permute-start(f32[2,1,16,128]{3,2,1,0:T(8,128)S(1)} %pad_maximum_fusion.27), channel_id=1, source_target_pairs={{0,1},{1,2},{2,3},{3,4},{4,5},{5,6},{6,7},{7,8},{8,9},{9,10},{10,1... | collective-permute-start | bytes 49160 | tf_op jit(solution)/shard_map/ppermute | solution.py:26
  456.8 5.3 %collective-permute-start.51 = (f32[2,1,16,128]{3,2,1,0:T(8,128)S(1)}, f32[2,1,16,128]{3,2,1,0:T(8,128)S(1)}, u32[]{:S(2)}, u32[]{:S(2)}) collective-permute-start(f32[2,1,16,128]{3,2,1,0:T(8,128)S(1)} %pad_maximum_fusion.25), channel_id=1, source_target_pairs={{0,1},{1,2},{2,3},{3,4},{4,5},{5,6},{6,7},{7,8},{8,9},{9,10},{10,1... | collective-permute-start | bytes 49160 | tf_op jit(solution)/shard_map/ppermute | solution.py:26
  465.4 5.3 %collective-permute-start.53 = (f32[2,1,16,128]{3,2,1,0:T(8,128)S(1)}, f32[2,1,16,128]{3,2,1,0:T(8,128)S(1)}, u32[]{:S(2)}, u32[]{:S(2)}) collective-permute-start(f32[2,1,16,128]{3,2,1,0:T(8,128)S(1)} %pad_maximum_fusion.23), channel_id=1, source_target_pairs={{0,1},{1,2},{2,3},{3,4},{4,5},{5,6},{6,7},{7,8},{8,9},{9,10},{10,1... | collective-permute-start | bytes 49160 | tf_op jit(solution)/shard_map/ppermute | solution.py:26
  474.0 5.3 %collective-permute-start.55 = (f32[2,1,16,128]{3,2,1,0:T(8,128)S(1)}, f32[2,1,16,128]{3,2,1,0:T(8,128)S(1)}, u32[]{:S(2)}, u32[]{:S(2)}) collective-permute-start(f32[2,1,16,128]{3,2,1,0:T(8,128)S(1)} %pad_maximum_fusion.21), channel_id=1, source_target_pairs={{0,1},{1,2},{2,3},{3,4},{4,5},{5,6},{6,7},{7,8},{8,9},{9,10},{10,1... | collective-permute-start | bytes 49160 | tf_op jit(solution)/shard_map/ppermute | solution.py:26
  482.6 5.6 %collective-permute-start.57 = (f32[2,1,16,128]{3,2,1,0:T(8,128)S(1)}, f32[2,1,16,128]{3,2,1,0:T(8,128)S(1)}, u32[]{:S(2)}, u32[]{:S(2)}) collective-permute-start(f32[2,1,16,128]{3,2,1,0:T(8,128)S(1)} %pad_maximum_fusion.19), channel_id=1, source_target_pairs={{0,1},{1,2},{2,3},{3,4},{4,5},{5,6},{6,7},{7,8},{8,9},{9,10},{10,1... | collective-permute-start | bytes 49160 | tf_op jit(solution)/shard_map/ppermute | solution.py:26
  491.5 6.2 %collective-permute-start.59 = (f32[2,1,16,128]{3,2,1,0:T(8,128)S(1)}, f32[2,1,16,128]{3,2,1,0:T(8,128)S(1)}, u32[]{:S(2)}, u32[]{:S(2)}) collective-permute-start(f32[2,1,16,128]{3,2,1,0:T(8,128)S(1)} %pad_maximum_fusion.17), channel_id=1, source_target_pairs={{0,1},{1,2},{2,3},{3,4},{4,5},{5,6},{6,7},{7,8},{8,9},{9,10},{10,1... | collective-permute-start | bytes 49160 | tf_op jit(solution)/shard_map/ppermute | solution.py:26
  (122 other events, 484.8 us)
where the time goes:
time: 533 us; the launch traced here: 530 us
  blocking collectives  178 us (33%)
  starting transfers between devices  176 us (33%)
  local copies, waits for them, and re-layouts  83.6 us (16%)
  waiting for transfers between devices  56.7 us (11%)
  other arithmetic  22.6 us (4%)
  matrix products  6.96 us (1%)
  between operations  6.81 us (1%)
    ppermute x60, starting transfers between devices, shifted(): return lax.ppermute(block, axis, route)  176 us
    psum x2, blocking collectives, body(): total_re, total_im = lax.psum((far_re, far_im), 'gx')  117 us
    psum x2, blocking collectives, body(): total = lax.psum(jnp.sum(gradient * gradient), 'gx')  60.9 us
    ppermute x60, waiting for transfers between devices, shifted(): return lax.ppermute(block, axis, route)  56.7 us
    gather x16, local copies, waits for them, and re-layouts, record_forward(): jnp.take(electric[1], slot_rows, axis=0)  17 us
    gather x15, local copies, waits for them, and re-layouts, record_forward(): jnp.take(magnetic[2], slot_rows, axis=0)  15.2 us
    gather x16, local copies, waits for them, and re-layouts, record_forward(): jnp.take(electric[2], slot_rows, axis=0)  15.2 us
    gather x15, local copies, waits for them, and re-layouts, record_forward(): jnp.take(magnetic[1], slot_rows, axis=0)  14.7 us
  transfers between devices with their start and end apart: 60, of which 52 were waited for; matrix products, arithmetic and copies ran while one was open for 15% of the time, Pallas kernels for 0%

commit v1 on v0

v1 whole, which is shorter than its diff:
```python
import functools
import math

import jax
import jax.numpy as jnp
import ml_dtypes
import numpy as np
from jax import lax
from jax.experimental import pallas as pl
from jax.experimental.pallas import tpu as pltpu
from jax.sharding import PartitionSpec as P

STEPS = 8
ITERS = 2
KY = 128
KZ = 16
PLANES_DEV = 2
COURANT = 0.5
OMEGA = 0.7
SPAN_EPS = 8.0
RATE = 0.5
EPSILON = 1e-06
HIGH = lax.Precision.HIGHEST
MESH = pl.DeviceIdType.MESH
GROUP = 16
CH = 4
F32 = jnp.float32


def split_table(table):
    high = table.astype(ml_dtypes.bfloat16)
    low = (table - high.astype(np.float64)).astype(ml_dtypes.bfloat16)
    return np.stack([high, low])


def make_tables(width, depth, rows, devices):
    angle = (np.arange(KY) + 0.5) * (math.pi / (2 * KY))
    wave_y = OMEGA / COURANT * np.sin(angle)
    wave_x = OMEGA / COURANT * np.cos(angle)
    wave_z = (np.arange(KZ) + 0.5) * (math.pi / KZ)
    phase_y = np.arange(width)[:, None] * wave_y[None, :]
    c, s = np.cos(phase_y), np.sin(phase_y)
    to_far = np.block([[c, -s], [s, c]])
    to_near = np.block([[c.T, -s.T], [s.T, c.T]])
    phase_z = wave_z[:, None] * np.arange(depth)[None, :]
    c, s = np.cos(phase_z), np.sin(phase_z)
    z_far = np.block([[c, s], [-s, c]])
    z_near = np.block([[c.T, s.T], [-s.T, c.T]])
    base = rows * np.arange(devices)[:, None] * wave_x[None, :]
    local = np.arange(-rows, 2 * rows)[:, None] * wave_x[None, :]
    times = np.arange(STEPS + 1) * OMEGA
    return (
        split_table(to_far),
        split_table(to_near),
        np.stack([z_far, z_near]).astype(np.float32),
        np.stack([np.cos(base), np.sin(base)]).astype(np.float32),
        np.stack([np.cos(local), np.sin(local)]).astype(np.float32),
        np.stack([np.cos(times), np.sin(times)]).astype(np.float32),
    )


def split(value):
    high = value.astype(jnp.bfloat16)
    return high, (value - high.astype(F32)).astype(jnp.bfloat16)


def dot3(left, table):
    high, low = split(left)
    out = jnp.dot(low, table[0], preferred_element_type=F32)
    out = out + jnp.dot(high, table[1], preferred_element_type=F32)
    return out + jnp.dot(high, table[0], preferred_element_type=F32)


def kernel(
    n, rows, depth, far_scale, near_scale, cells_total,
    e_in, h_in, bg_in, de_in, ma_in, counts, slots, cells, amps, target,
    to_far, to_near, z_tab, x_base, x_local, time_tab,
    new_out, final_out, far_out,
    eh, hh, bg, de, ma, marks, inv, src, ae, ah, adj, sens, grads, phase,
    part, gathered, reduced, crossed, summed, norms, norm_cross, mine,
    local_sem, halo_send, halo_recv, grad_send, grad_recv,
    rs_send, rs_recv, ag_send, ag_recv, no_send, no_recv, x_send, x_recv, xn_send, xn_recv,
):
    me = lax.axis_index("gx")
    own_part = lax.axis_index("parts")
    groups = n // GROUP
    loc = lax.rem(me, GROUP)
    grp = me // GROUP
    first = grp * GROUP
    block = rows * depth
    wide = 3 * block
    width = bg_in.shape[-1]
    has_left = me > 0
    has_right = me < n - 1
    OWN = pl.ds(block, block)
    ghost = (pl.ds(0, block), pl.ds(2 * block, block))

    def device(index):
        return (own_part, index)

    barrier = pltpu.get_barrier_semaphore()
    for d in range(1, GROUP):
        pl.semaphore_signal(
            barrier, inc=1, device_id=device(first + lax.rem(loc + d, GROUP)), device_id_type=MESH
        )
    for d in range(1, groups):
        pl.semaphore_signal(
            barrier, inc=1, device_id=device(lax.rem(me + d * GROUP, n)), device_id_type=MESH
        )
    greetings = GROUP - 1 + groups - 1
    if groups > 1:
        outer_left = has_left & (loc == 0)
        outer_right = has_right & (loc == GROUP - 1)

        @pl.when(outer_left)
        def _():
            pl.semaphore_signal(barrier, inc=1, device_id=device(me - 1), device_id_type=MESH)

        @pl.when(outer_right)
        def _():
            pl.semaphore_signal(barrier, inc=1, device_id=device(me + 1), device_id_type=MESH)

        greetings = greetings + outer_left.astype(jnp.int32) + outer_right.astype(jnp.int32)

    moves = [
        pltpu.make_async_copy(e_in, eh.at[0, :, OWN], local_sem.at[0]),
        pltpu.make_async_copy(h_in, hh.at[0, :, OWN], local_sem.at[1]),
        pltpu.make_async_copy(bg_in, bg.at[OWN], local_sem.at[2]),
        pltpu.make_async_copy(de_in, de.at[OWN], local_sem.at[3]),
        pltpu.make_async_copy(ma_in, ma.at[OWN], local_sem.at[4]),
    ]
    for move in moves:
        move.start()

    row_of = lax.broadcasted_iota(jnp.int32, (rows, width), 0)
    mark = jnp.zeros((rows, width), F32)
    for s in range(slots.shape[1]):
        mark = mark + jnp.where((row_of == slots[0, s]) & (s < counts[0]), 1.0, 0.0)
    marks[1] = mark

    pl.semaphore_wait(barrier, greetings)

    def halo(side):
        other = device(jnp.clip(me + (1 if side == 0 else -1), 0, n - 1))
        where = ghost[side]
        pairs = [
            (e_in, eh.at[0, :, where]),
            (h_in, hh.at[0, :, where]),
            (bg_in, bg.at[where]),
            (de_in, de.at[where]),
            (ma_in, ma.at[where]),
            (marks.at[1], marks.at[2 * side]),
        ]
        return [
            pltpu.make_async_remote_copy(
                src_ref=a, dst_ref=b, send_sem=halo_send.at[side, i], recv_sem=halo_recv.at[side, i],
                device_id=other, device_id_type=MESH,
            )
            for i, (a, b) in enumerate(pairs)
        ]

    def grad_halo(side):
        other = device(jnp.clip(me + (1 if side == 0 else -1), 0, n - 1))
        return pltpu.make_async_remote_copy(
            src_ref=grads.at[OWN], dst_ref=grads.at[ghost[side]],
            send_sem=grad_send.at[side], recv_sem=grad_recv.at[side],
            device_id=other, device_id_type=MESH,
        )

    sends = (has_right, has_left)
    comes = (has_left, has_right)
    for side in (0, 1):

        @pl.when(sends[side])
        def _():
            for copy in halo(side):
                copy.start()

        @pl.when(jnp.logical_not(comes[side]))
        def _():
            where = ghost[side]
            eh[0, :, where] = jnp.zeros((3, block, width), F32)
            hh[0, :, where] = jnp.zeros((3, block, width), F32)
            bg[where] = jnp.ones((block, width), F32)
            de[where] = jnp.zeros((block, width), F32)
            ma[where] = jnp.zeros((block, width), jnp.int32)
            marks[2 * side] = jnp.zeros((rows, width), F32)
            grads[where] = jnp.zeros((block, width), F32)

    ids = cells[...] - (me - 1) * block * width
    line = lax.broadcasted_iota(jnp.int32, (wide, ids.shape[1]), 0)
    lane = lax.broadcasted_iota(jnp.int32, (width, ids.shape[1]), 0)
    place = lax.shift_right_arithmetic(ids, width.bit_length() - 1)
    rest = jnp.bitwise_and(ids, width - 1)
    left = jnp.where(line == place, amps[...], 0.0)
    right = jnp.where(lane == rest, 1.0, 0.0)
    src[...] = lax.dot_general(
        left, right, (((1,), (1,)), ((), ())), precision=HIGH, preferred_element_type=F32
    )

    base_c, base_s = x_base[0, pl.ds(me, 1), :], x_base[1, pl.ds(me, 1), :]
    phase[0] = base_c * x_local[0] - base_s * x_local[1]
    phase[1] = base_s * x_local[0] + base_c * x_local[1]

    for move in moves:
        move.wait()
    for side in (0, 1):

        @pl.when(comes[side])
        def _():
            for copy in halo(side):
                copy.wait_recv()

    span = CH * depth
    y_at = lax.broadcasted_iota(jnp.int32, (span, width), 1)
    z_at = lax.rem(lax.broadcasted_iota(jnp.int32, (span, width), 0), depth)
    y_last, y_first = y_at == width - 1, y_at == 0
    z_last, z_first = z_at == depth - 1, z_at == 0

    def up_y(f):
        return jnp.where(y_last, 0.0, pltpu.roll(f, width - 1, 1)) - f

    def up_z(f):
        return jnp.where(z_last, 0.0, pltpu.roll(f, span - 1, 0)) - f

    def down_y(f):
        return f - jnp.where(y_first, 0.0, pltpu.roll(f, 1, 1))

    def down_z(f):
        return f - jnp.where(z_first, 0.0, pltpu.roll(f, 1, 0))

    def behind(edge, f):
        return jnp.concatenate([edge, f[: span - depth]], axis=0)

    def sweep(t, load_e, load_h, store_e, store_h, drive):
        chunks = 3 * rows // CH

        def chunk(c, carry):
            prev_y, prev_z = carry
            at = pl.ds(pl.multiple_of(c * span, span), span)
            ahead = pl.ds(pl.multiple_of(c * span + depth, depth), span)
            ch = jnp.where(has_left | (c >= rows // CH), COURANT, 0.0).astype(F32)
            ex, ey, ez = (load_e(i, at) for i in range(3))
            hx = load_h(0, at) - ch * (up_y(ez) - up_z(ey))
            hy = load_h(1, at) - ch * (up_z(ex) - (load_e(2, ahead) - ez))
            hz = load_h(2, at) - ch * ((load_e(1, ahead) - ey) - up_y(ex))
            store_h(0, at, hx)
            store_h(1, at, hy)
            store_h(2, at, hz)
            scale = inv[at]
            add_y, add_z = drive(at)
            nx = ex + scale * (down_y(hz) - down_z(hy))
            ny = ey + scale * (down_z(hx) - (hz - behind(prev_z, hz)))
            nz = ez + scale * ((hy - behind(prev_y, hy)) - down_y(hx)) + add_z
            if add_y is not None:
                ny = ny + add_y
            store_e(0, at, nx)
            store_e(1, at, ny)
            store_e(2, at, nz)
            return hy[span - depth :], hz[span - depth :]

        low = (t - 1) // CH
        high = (3 * rows - t + CH - 1) // CH
        zero = jnp.zeros((depth, width), F32)
        lax.fori_loop(low, jnp.minimum(high, chunks), chunk, (zero, zero))

    def forward(t, _):
        def load(ref):
            return lambda i, at: ref[t - 1, i, at]

        def store(ref):
            def put(i, at, value):
                ref[t, i, at] = value

            return put

        wave = time_tab[1, t]
        sweep(t, load(eh), load(hh), store(eh), store(hh), lambda at: (None, wave * src[at]))
        return 0

    def adjoint(tau, _):
        t = STEPS + 1 - tau
        cos_t, sin_t = time_tab[0, t], time_tab[1, t]

        def load(ref):
            return lambda i, at: ref[i, at]

        def store(ref):
            def put(i, at, value):
                ref[i, at] = value

            return put

        def drive(at):
            return tuple(cos_t * adj[2 * f, at] + sin_t * adj[2 * f + 1, at] for f in (0, 1))

        sweep(tau, load(ae), load(ah), store(ae), store(ah), drive)
        add_sensitivity(t)
        return 0

    def add_sensitivity(t):
        for c in range(rows // CH):
            at, here = pl.ds(c * span, span), pl.ds(block + c * span, span)
            total = sens[at]
            for i in range(3):
                total = total + eh[t, i, here] * ae[i, here]
            sens[at] = total

    def peers(copy_of):
        return [copy_of(lax.rem(loc + d, GROUP), d) for d in range(1, GROUP)]

    def remote(src_ref, dst_ref, send, recv, target_device):
        return pltpu.make_async_remote_copy(
            src_ref=src_ref, dst_ref=dst_ref, send_sem=send, recv_sem=recv,
            device_id=device(target_device), device_id_type=MESH,
        )

    def exchange(out, landing):
        for copy in out:
            copy.start()
        for copy in landing:
            copy.wait_recv()
        for copy in out:
            copy.wait_send()

    def across(value, buffer, send, recv):
        if groups == 1:
            return value
        buffer[grp] = value
        out = [
            remote(buffer.at[grp], buffer.at[grp], send.at[d], recv.at[grp], lax.rem(me + d * GROUP, n))
            for d in range(1, groups)
        ]
        landing = []
        for d in range(1, groups):
            there = lax.rem(grp + d, groups)
            landing.append(remote(buffer.at[there], buffer.at[there], send.at[d], recv.at[there], me))
        exchange(out, landing)
        total = buffer[0]
        for g in range(1, groups):
            total = total + buffer[g]
        return total

    def reduce_far():
        out = peers(lambda p, d: remote(part.at[p], reduced.at[loc], rs_send.at[d], rs_recv.at[loc], first + p))
        landing = peers(lambda p, d: remote(part.at[p], reduced.at[p], rs_send.at[d], rs_recv.at[p], first + p))
        reduced[loc] = part[loc]
        exchange(out, landing)
        total = reduced[0]
        for i in range(1, GROUP):
            total = total + reduced[i]
        gathered[loc] = across(total, crossed, x_send, x_recv)
        out = peers(lambda p, d: remote(gathered.at[loc], gathered.at[loc], ag_send.at[d], ag_recv.at[loc], first + p))
        landing = peers(lambda p, d: remote(gathered.at[p], gathered.at[p], ag_send.at[d], ag_recv.at[p], first + p))
        exchange(out, landing)

    def reduce_norm(tile):
        norms[loc] = tile
        out = peers(lambda p, d: remote(norms.at[loc], norms.at[loc], no_send.at[d], no_recv.at[loc], first + p))
        landing = peers(lambda p, d: remote(norms.at[p], norms.at[p], no_send.at[d], no_recv.at[p], first + p))
        exchange(out, landing)
        total = norms[0]
        for i in range(1, GROUP):
            total = total + norms[i]
        total = across(total, norm_cross, xn_send, xn_recv)
        return jnp.sum(jnp.sum(total, axis=0, keepdims=True), axis=1, keepdims=True)

    lines = KZ // 4
    for iteration in range(ITERS):
        last = iteration == ITERS - 1
        for c in range(3):
            at = pl.ds(c * block, block)
            squash = 1.0 / (1.0 + jnp.exp(-de[at]))
            scale = COURANT / (bg[at] + SPAN_EPS * ma[at].astype(F32) * squash)
            if c != 1:
                scale = jnp.where(comes[0] if c == 0 else comes[1], scale, 0.0)
            inv[at] = scale
        lax.fori_loop(1, STEPS + 1, forward, 0)
        if last:
            final = pltpu.make_async_copy(eh.at[STEPS, :, OWN], final_out, local_sem.at[0])
            final.start()

        for f in (0, 1):
            far_re = jnp.zeros((depth, KY), F32)
            far_im = jnp.zeros((depth, KY), F32)
            re_rows, im_rows = [], []
            for r in range(rows):
                at = pl.ds(block + r * depth, depth)
                mon_re = jnp.zeros((depth, width), F32)
                mon_im = jnp.zeros((depth, width), F32)
                for t in range(1, STEPS + 1):
                    plane = eh[t, 1, at] + hh[t, 2, at] if f == 0 else eh[t, 2, at] - hh[t, 1, at]
                    mon_re = mon_re + math.cos(OMEGA * t) * plane
                    mon_im = mon_im - math.sin(OMEGA * t) * plane
                re_rows.append(mon_re)
                im_rows.append(mon_im)
            stacked = jnp.concatenate(
                [jnp.concatenate(re_rows, axis=0), jnp.concatenate(im_rows, axis=0)], axis=1
            )
            flat = dot3(stacked, to_far)
            for r in range(rows):
                valid = marks[1, r : r + 1, :]
                cos_x = phase[0, rows + r : rows + r + 1, :] * valid
                sin_x = phase[1, rows + r : rows + r + 1, :] * valid
                y_re = flat[r * depth : (r + 1) * depth, :KY]
                y_im = flat[r * depth : (r + 1) * depth, KY:]
                far_re = far_re + cos_x * y_re + sin_x * y_im
                far_im = far_im + cos_x * y_im - sin_x * y_re
            far = far_scale * jnp.dot(
                z_tab[0], jnp.concatenate([far_re, far_im], axis=0), precision=HIGH, preferred_element_type=F32
            )
            for i in range(8):
                part[8 * f + i] = far[lines * i : lines * (i + 1)]
        reduce_far()

        power = jnp.zeros((KZ, KY), F32)
        for f in (0, 1):
            total = jnp.concatenate([gathered[8 * f + i] for i in range(8)], axis=0)
            total_re, total_im = total[:KZ], total[KZ:]
            power = power + total_re * total_re + total_im * total_im
            weight = jnp.concatenate([2.0 * target[...] * total_re, -2.0 * target[...] * total_im], axis=0)
            zed = near_scale * jnp.dot(z_tab[1], weight, precision=HIGH, preferred_element_type=F32)
            zed_re, zed_im = zed[:depth], zed[depth:]
            for side in range(3):
                slot = []
                for r in range(rows):
                    x = side * rows + r
                    valid = marks[side, r : r + 1, :]
                    cos_x = phase[0, x : x + 1, :] * valid
                    sin_x = phase[1, x : x + 1, :] * valid
                    slot.append(
                        jnp.concatenate(
                            [cos_x * zed_re + sin_x * zed_im, cos_x * zed_im - sin_x * zed_re], axis=1
                        )
                    )
                near = dot3(jnp.concatenate(slot, axis=0), to_near)
                at = pl.ds(side * block, block)
                adj[2 * f, at] = near[:, :width]
                adj[2 * f + 1, at] = near[:, width:]
                ae[f + 1, at] = (
                    math.cos(OMEGA * STEPS) * near[:, :width] + math.sin(OMEGA * STEPS) * near[:, width:]
                )
        if last:
            far_out[...] = power
        ae[0] = jnp.zeros(ae.shape[1:], F32)
        ah[...] = jnp.zeros(ah.shape, F32)
        sens[...] = jnp.zeros(sens.shape, F32)
        add_sensitivity(STEPS)
        lax.fori_loop(2, STEPS + 1, adjoint, 0)

        squash = 1.0 / (1.0 + jnp.exp(-de[OWN]))
        gradient = sens[...] * ma[OWN].astype(F32) * SPAN_EPS * squash * (1.0 - squash)
        grads[OWN] = gradient
        if not last:
            for side in (0, 1):

                @pl.when(sends[side])
                def _():
                    grad_halo(side).start()

        square = gradient * gradient
        tile = square[:8]
        for i in range(1, block // 8):
            tile = tile + square[8 * i : 8 * (i + 1)]
        factor = RATE / jnp.sqrt(reduce_norm(tile) / cells_total + EPSILON)
        if last:
            new_out[...] = de[OWN] + factor * gradient
        else:
            for side in (0, 1):

                @pl.when(comes[side])
                def _():
                    grad_halo(side).wait_recv()

            de[...] = de[...] + factor * grads[...]
            for side in (0, 1):

                @pl.when(sends[side])
                def _():
                    grad_halo(side).wait_send()

    for side in (0, 1):

        @pl.when(sends[side])
        def _():
            for copy in halo(side):
                copy.wait_send()

    final.wait()


def body(n, e_start, h_start, background, design, design_mask, plane_counts, plane_rows, source_cells, source_amp, target):
    rows, depth, width = background.shape
    block = rows * depth
    groups = n // GROUP
    tables = make_tables(width, depth, rows, n)
    far_scale = 1.0 / math.sqrt(width * depth * PLANES_DEV * n * STEPS)
    near_scale = 1.0 / math.sqrt(KY * KZ)
    vmem = pl.BlockSpec(memory_space=pltpu.VMEM)
    smem = pl.BlockSpec(memory_space=pltpu.SMEM)
    hbm = pl.BlockSpec(memory_space=pl.ANY)
    dma = pltpu.SemaphoreType.DMA
    fields = (3, 3 * block + depth, width)
    new_design, final_field, intensity = pl.pallas_call(
        functools.partial(
            kernel, n, rows, depth, far_scale, near_scale, float(rows * n * depth * width)
        ),
        out_shape=(
            jax.ShapeDtypeStruct((block, width), F32),
            jax.ShapeDtypeStruct((3, block, width), F32),
            jax.ShapeDtypeStruct((KZ, KY), F32),
        ),
        in_specs=[hbm] * 5 + [smem] * 2 + [vmem] * 8 + [smem],
        out_specs=(vmem, hbm, vmem),
        scratch_shapes=[
            pltpu.VMEM((STEPS + 1,) + fields, F32),
            pltpu.VMEM((STEPS + 1,) + fields, F32),
            pltpu.VMEM((3 * block, width), F32),
            pltpu.VMEM((3 * block, width), F32),
            pltpu.VMEM((3 * block, width), jnp.int32),
            pltpu.VMEM((3, rows, width), F32),
            pltpu.VMEM((3 * block, width), F32),
            pltpu.VMEM((3 * block, width), F32),
            pltpu.VMEM(fields, F32),
            pltpu.VMEM(fields, F32),
            pltpu.VMEM((4, 3 * block, width), F32),
            pltpu.VMEM((block, width), F32),
            pltpu.VMEM((3 * block, width), F32),
            pltpu.VMEM((2, 3 * rows, width), F32),
            pltpu.VMEM((GROUP, KZ // 4, KY), F32),
            pltpu.VMEM((GROUP, KZ // 4, KY), F32),
            pltpu.VMEM((GROUP, KZ // 4, KY), F32),
            pltpu.VMEM((groups, KZ // 4, KY), F32),
            pltpu.VMEM((KZ // 4, KY), F32),
            pltpu.VMEM((GROUP, 8, width), F32),
            pltpu.VMEM((groups, 8, width), F32),
            pltpu.VMEM((8, width), F32),
            dma((5,)),
            dma((2, 6)),
            dma((2, 6)),
            dma((2,)),
            dma((2,)),
        ]
        + [dma((GROUP,))] * 6
        + [dma((groups,))] * 4,
        compiler_params=pltpu.CompilerParams(
            collective_id=0, has_side_effects=True, vmem_limit_bytes=40 * 1024 * 1024
        ),
    )(
        e_start.reshape(3, block, width),
        h_start.reshape(3, block, width),
        background.reshape(block, width),
        design.reshape(block, width),
        design_mask.reshape(block, width),
        plane_counts,
        plane_rows,
        source_cells.reshape(1, -1),
        source_amp.reshape(1, -1),
        target,
        *tables,
    )
    return (
        new_design.reshape(rows, depth, width),
        final_field.reshape(3, rows, depth, width),
        intensity,
    )


def solution(mesh):
    return jax.shard_map(
        functools.partial(body, mesh.shape["gx"]),
        mesh=mesh,
        in_specs=(
            P(None, ("parts", "gx"), None, None),
            P(None, ("parts", "gx"), None, None),
            P(("parts", "gx"), None, None),
            P(("parts", "gx"), None, None),
            P(("parts", "gx"), None, None),
            P(("parts", "gx")),
            P(("parts", "gx"), None),
            P("parts"),
            P("parts"),
            P(),
        ),
        out_specs=(
            P(("parts", "gx"), None, None),
            P(None, ("parts", "gx"), None, None),
            P("parts", None),
        ),
        check_vma=False,
    )
```

time: 533 us -> 88 us (0.17)
  blocking collectives: 178 us -> 0 us
  starting transfers between devices: 176 us -> 0 us
  Pallas kernels: 0 us -> 75 us
  local copies, waits for them, and re-layouts: 83.6 us -> 11 us
  waiting for transfers between devices: 56.7 us -> 0 us
  other arithmetic: 22.6 us -> 0 us
  matrix products: 6.96 us -> 0 us
  between operations: 6.81 us -> 1.36 us
    psum x4 -> x0, blocking collectives: 178 us -> none  [the longest x2 117 us: body(): total_re, total_im = lax.psum((far_re, far_im), 'gx')]
    ppermute x60 -> x0, starting transfers between devices: 176 us -> none  [shifted(): return lax.ppermute(block, axis, route)]
    pallas_call x0 -> x1, Pallas kernels: none -> 75 us  [body(): pl.pallas_call(functools.partial(kernel, n, rows, depth, far_scale, near_...]
    gather x62 -> x0, local copies, waits for them, and re-layouts: 62.2 us -> none  [the longest x16 17 us: record_forward(): jnp.take(electric[1], slot_rows, axis=0)]
    ppermute x60 -> x0, waiting for transfers between devices: 56.7 us -> none  [shifted(): return lax.ppermute(block, axis, route)]
    slice x234 -> x0, local copies, waits for them, and re-layouts: 7.81 us -> none  [the longest x116 5.18 us: forward_diff(): lax.slice_in_dim(field, 1, length, axis=axis)]
    dot_general x20 -> x0, matrix products: 6.96 us -> none  [the longest x2 0.78 us: project(): jnp.einsum('fszk,zm->fsmk', part_re, sin_z, precision=HIGH)]
    unnamed x188 -> x33, local copies, waits for them, and re-layouts: 11.1 us -> 11 us
  transfers between devices with their start and end apart: 60 -> 0, of which waited for: 52 -> 0; matrix products, arithmetic and copies ran while one was open for 15% -> 0% of each run, Pallas kernels for 0% -> 0%
where the time goes in v1:
time: 88 us; the launch traced here: 87.4 us
  Pallas kernels  75 us (85%)
  local copies, waits for them, and re-layouts  11 us (12%)
  between operations  1.36 us (2%)
    pallas_call x1, Pallas kernels, body(): pl.pallas_call(functools.partial(kernel, n, rows, depth, far_scale, near_...  75 us
    unnamed x33, local copies, waits for them, and re-layouts  11 us

profile of v1, /device:TPU:0, one launch (start us, length us, event | category | flops | bytes accessed | tf_op | source)
XLA Modules:
  0.0 87.4 jit_solution(4249680995977370462)
XLA Ops:
  0.6 0.0 copy-start.9
  1.3 0.0 copy-start.13
  1.3 0.0 copy-start.14
  1.3 0.0 copy-start.11
  1.3 0.0 copy-start.12
  1.3 0.0 copy-done.9
  1.4 0.6 copy-done.13
  2.0 0.0 copy-done.14
  2.0 0.0 copy-done.11
  2.0 0.0 copy-done.12
  2.0 0.0 copy-start
  2.0 0.9 %copy-done = bf16[2,256,256]{2,1,0:T(8,128)(2,1)S(1)} copy-done((bf16[2,256,256]{2,1,0:T(8,128)(2,1)S(1)}, bf16[2,256,256]{2,1,0:T(8,128)(2,1)}, u32[]{:S(2)}) %copy-start) | copy-done | bytes 262168
  3.0 0.0 copy-start.1
  3.0 0.9 %copy-done.1 = bf16[2,256,256]{2,1,0:T(8,128)(2,1)S(1)} copy-done((bf16[2,256,256]{2,1,0:T(8,128)(2,1)S(1)}, bf16[2,256,256]{2,1,0:T(8,128)(2,1)}, u32[]{:S(2)}) %copy-start.1) | copy-done | bytes 262168
  3.9 0.0 copy-start.2
  3.9 0.9 %copy-done.2 = f32[3,8,16,128]{3,2,1,0:T(8,128)S(1)} copy-done((f32[3,8,16,128]{3,2,1,0:T(8,128)S(1)}, f32[3,8,16,128]{3,2,1,0:T(8,128)}, u32[]{:S(2)}) %copy-start.2) | copy-done | bytes 196632
  4.8 0.0 copy-start.3
  4.9 0.9 %copy-done.3 = f32[3,8,16,128]{3,2,1,0:T(8,128)S(1)} copy-done((f32[3,8,16,128]{3,2,1,0:T(8,128)S(1)}, f32[3,8,16,128]{3,2,1,0:T(8,128)}, u32[]{:S(2)}) %copy-start.3) | copy-done | bytes 196632
  5.8 0.0 copy-start.4
  5.8 0.8 copy-done.4
  6.6 0.0 copy-start.5
  6.6 0.8 copy-done.5
  7.5 0.0 copy-start.6
  7.5 0.8 copy-done.6
  8.3 0.0 copy-start.7
  8.3 0.8 copy-done.7
  9.1 0.7 copy-done.8
  9.8 0.7 copy-done.10
  10.5 75.0 %shard_map.175 = (f32[128,128]{1,0:T(8,128)S(1)}, f32[3,128,128]{2,1,0:T(8,128)S(1)}, f32[16,128]{1,0:T(8,128)S(1)}) custom-call(f32[3,128,128]{2,1,0:T(8,128)S(1)} %bitcast.10, f32[3,128,128]{2,1,0:T(8,128)S(1)} %bitcast.11, f32[128,128]{1,0:T(8,128)S(1)} %bitcast.13, f32[128,128]{1,0:T(8,128)S(1)} %bitcast.14, s32[128,128]{1,0:T(8,128)S(1)} %bitcast.15, ...), custom_call_target="tpu_custom_call" | custom-call | tf_op jit(solution)/shard_map/pallas_call | solution.py:504
  85.5 0.6 copy.23
  86.2 0.7 copy.24
  86.8 0.6 copy.25
  (2 shorter events, 0.0 us)
Async XLA Ops:
  0.6 0.7 copy-start.9
  1.3 0.7 copy-start.13
  1.3 0.7 copy-start.14
  1.3 0.7 copy-start.11
  1.3 0.7 copy-start.12
  2.0 1.0 %copy-start = (bf16[2,256,256]{2,1,0:T(8,128)(2,1)S(1)}, bf16[2,256,256]{2,1,0:T(8,128)(2,1)}, u32[]{:S(2)}) copy-start(bf16[2,256,256]{2,1,0:T(8,128)(2,1)} %constant.13.clone.to_near) | copy-start | bytes 786436
  3.0 0.9 %copy-start.1 = (bf16[2,256,256]{2,1,0:T(8,128)(2,1)S(1)}, bf16[2,256,256]{2,1,0:T(8,128)(2,1)}, u32[]{:S(2)}) copy-start(bf16[2,256,256]{2,1,0:T(8,128)(2,1)} %constant.12.clone.to_far) | copy-start | bytes 786436
  3.9 0.9 %copy-start.2 = (f32[3,8,16,128]{3,2,1,0:T(8,128)S(1)}, f32[3,8,16,128]{3,2,1,0:T(8,128)}, u32[]{:S(2)}) copy-start(f32[3,8,16,128]{3,2,1,0:T(8,128)} %param.16) | copy-start | bytes 589828
  4.8 0.9 %copy-start.3 = (f32[3,8,16,128]{3,2,1,0:T(8,128)S(1)}, f32[3,8,16,128]{3,2,1,0:T(8,128)}, u32[]{:S(2)}) copy-start(f32[3,8,16,128]{3,2,1,0:T(8,128)} %param.17) | copy-start | bytes 589828
  5.8 0.8 copy-start.4
  6.6 0.8 copy-start.5
  7.5 0.8 copy-start.6
  8.3 0.8 copy-start.7
  9.1 0.7 copy-start.8
  9.8 0.7 copy-start.10

commit v2 on v1

--- a/solution.py
+++ b/solution.py
@@ -23,7 +23,7 @@
 HIGH = lax.Precision.HIGHEST
 MESH = pl.DeviceIdType.MESH
 GROUP = 16
-CH = 4
+CH = 8
 F32 = jnp.float32
 
 
@@ -48,15 +48,19 @@
     z_near = np.block([[c.T, s.T], [-s.T, c.T]])
     base = rows * np.arange(devices)[:, None] * wave_x[None, :]
     local = np.arange(-rows, 2 * rows)[:, None] * wave_x[None, :]
-    times = np.arange(STEPS + 1) * OMEGA
+    along = np.concatenate([local, base])
     return (
-        split_table(to_far),
-        split_table(to_near),
+        np.concatenate([split_table(to_far), split_table(to_near)]),
         np.stack([z_far, z_near]).astype(np.float32),
-        np.stack([np.cos(base), np.sin(base)]).astype(np.float32),
-        np.stack([np.cos(local), np.sin(local)]).astype(np.float32),
-        np.stack([np.cos(times), np.sin(times)]).astype(np.float32),
+        np.stack([np.cos(along), np.sin(along)]).astype(np.float32),
     )
+
+
+def at_time(function, t):
+    value = jnp.where(t == 1, function(OMEGA), 0.0).astype(F32)
+    for k in range(2, STEPS + 1):
+        value = jnp.where(t == k, function(OMEGA * k), value).astype(F32)
+    return value
 
 
 def split(value):
@@ -64,20 +68,31 @@
     return high, (value - high.astype(F32)).astype(jnp.bfloat16)
 
 
-def dot3(left, table):
+def dot3(left, table, i):
     high, low = split(left)
-    out = jnp.dot(low, table[0], preferred_element_type=F32)
-    out = out + jnp.dot(high, table[1], preferred_element_type=F32)
-    return out + jnp.dot(high, table[0], preferred_element_type=F32)
+    out = jnp.dot(low, table[i], preferred_element_type=F32)
+    out = out + jnp.dot(high, table[i + 1], preferred_element_type=F32)
+    return out + jnp.dot(high, table[i], preferred_element_type=F32)
 
 
 def kernel(
     n, rows, depth, far_scale, near_scale, cells_total,
-    e_in, h_in, bg_in, de_in, ma_in, counts, slots, cells, amps, target,
-    to_far, to_near, z_tab, x_base, x_local, time_tab,
+    e_in, h_in, bg_in, de_in, ma_in, *rest,
+):
+    small_in, (new_out, final_out, far_out), rest = rest[:8], rest[8:11], rest[11:]
+    small, rest = rest[:8], rest[8:]
+    run(
+        n, rows, depth, far_scale, near_scale, cells_total, e_in, h_in, bg_in, de_in, ma_in,
+        small_in, *small, new_out, final_out, far_out, *rest,
+    )
+
+
+def run(
+    n, rows, depth, far_scale, near_scale, cells_total, e_in, h_in, bg_in, de_in, ma_in,
+    small_in, counts, slots, cells, amps, target, y_tab, z_tab, x_tab,
     new_out, final_out, far_out,
     eh, hh, bg, de, ma, marks, inv, src, ae, ah, adj, sens, grads, phase,
-    part, gathered, reduced, crossed, summed, norms, norm_cross, mine,
+    part, gathered, reduced, crossed, norms, norm_cross, new_own, power_own,
     local_sem, halo_send, halo_recv, grad_send, grad_recv,
     rs_send, rs_recv, ag_send, ag_recv, no_send, no_recv, x_send, x_recv, xn_send, xn_recv,
 ):
@@ -129,14 +144,19 @@
         pltpu.make_async_copy(de_in, de.at[OWN], local_sem.at[3]),
         pltpu.make_async_copy(ma_in, ma.at[OWN], local_sem.at[4]),
     ]
-    for move in moves:
+    loads = [
+        pltpu.make_async_copy(a, b, local_sem.at[5 + i])
+        for i, (a, b) in enumerate(zip(small_in, (counts, slots, cells, amps, target, y_tab, z_tab, x_tab)))
+    ]
+    for move in loads + moves:
         move.start()
-
-    row_of = lax.broadcasted_iota(jnp.int32, (rows, width), 0)
-    mark = jnp.zeros((rows, width), F32)
-    for s in range(slots.shape[1]):
-        mark = mark + jnp.where((row_of == slots[0, s]) & (s < counts[0]), 1.0, 0.0)
-    marks[1] = mark
+    for move in loads:
+        move.wait()
+
+    at_row = lax.broadcasted_iota(jnp.int32, (rows, slots.shape[1]), 0)
+    at_slot = lax.broadcasted_iota(jnp.int32, (rows, slots.shape[1]), 1)
+    hit = jnp.where((at_row == slots[...]) & (at_slot < counts[...]), 1.0, 0.0)
+    marks[1] = jnp.broadcast_to(jnp.sum(hit, axis=1, keepdims=True), (rows, width))
 
     pl.semaphore_wait(barrier, greetings)
 
@@ -198,9 +218,10 @@
         left, right, (((1,), (1,)), ((), ())), precision=HIGH, preferred_element_type=F32
     )
 
-    base_c, base_s = x_base[0, pl.ds(me, 1), :], x_base[1, pl.ds(me, 1), :]
-    phase[0] = base_c * x_local[0] - base_s * x_local[1]
-    phase[1] = base_s * x_local[0] + base_c * x_local[1]
+    base_c, base_s = (x_tab[i, pl.ds(3 * rows + me, 1), :] for i in (0, 1))
+    near_c, near_s = (x_tab[i, : 3 * rows, :] for i in (0, 1))
+    phase[0] = base_c * near_c - base_s * near_s
+    phase[1] = base_s * near_c + base_c * near_s
 
     for move in moves:
         move.wait()
@@ -274,13 +295,13 @@
 
             return put
 
-        wave = time_tab[1, t]
+        wave = at_time(math.sin, t)
         sweep(t, load(eh), load(hh), store(eh), store(hh), lambda at: (None, wave * src[at]))
         return 0
 
     def adjoint(tau, _):
         t = STEPS + 1 - tau
-        cos_t, sin_t = time_tab[0, t], time_tab[1, t]
+        cos_t, sin_t = at_time(math.cos, t), at_time(math.sin, t)
 
         def load(ref):
             return lambda i, at: ref[i, at]
@@ -320,8 +341,14 @@
             copy.start()
         for copy in landing:
             copy.wait_recv()
-        for copy in out:
+        pending.extend(out)
+
+    pending = []
+
+    def settle():
+        for copy in pending:
             copy.wait_send()
+        pending.clear()
 
     def across(value, buffer, send, recv):
         if groups == 1:
@@ -366,6 +393,7 @@
         return jnp.sum(jnp.sum(total, axis=0, keepdims=True), axis=1, keepdims=True)
 
     lines = KZ // 4
+    results = []
     for iteration in range(ITERS):
         last = iteration == ITERS - 1
         for c in range(3):
@@ -377,8 +405,8 @@
             inv[at] = scale
         lax.fori_loop(1, STEPS + 1, forward, 0)
         if last:
-            final = pltpu.make_async_copy(eh.at[STEPS, :, OWN], final_out, local_sem.at[0])
-            final.start()
+            results.append(pltpu.make_async_copy(eh.at[STEPS, :, OWN], final_out, local_sem.at[0]))
+            results[-1].start()
 
         for f in (0, 1):
             far_re = jnp.zeros((depth, KY), F32)
@@ -397,7 +425,7 @@
             stacked = jnp.concatenate(
                 [jnp.concatenate(re_rows, axis=0), jnp.concatenate(im_rows, axis=0)], axis=1
             )
-            flat = dot3(stacked, to_far)
+            flat = dot3(stacked, y_tab, 0)
             for r in range(rows):
                 valid = marks[1, r : r + 1, :]
                 cos_x = phase[0, rows + r : rows + r + 1, :] * valid
@@ -433,7 +461,7 @@
                             [cos_x * zed_re + sin_x * zed_im, cos_x * zed_im - sin_x * zed_re], axis=1
                         )
                     )
-                near = dot3(jnp.concatenate(slot, axis=0), to_near)
+                near = dot3(jnp.concatenate(slot, axis=0), y_tab, 2)
                 at = pl.ds(side * block, block)
                 adj[2 * f, at] = near[:, :width]
                 adj[2 * f + 1, at] = near[:, width:]
@@ -441,12 +469,15 @@
                     math.cos(OMEGA * STEPS) * near[:, :width] + math.sin(OMEGA * STEPS) * near[:, width:]
                 )
         if last:
-            far_out[...] = power
+            power_own[...] = power
+            results.append(pltpu.make_async_copy(power_own, far_out, local_sem.at[2]))
+            results[-1].start()
         ae[0] = jnp.zeros(ae.shape[1:], F32)
         ah[...] = jnp.zeros(ah.shape, F32)
         sens[...] = jnp.zeros(sens.shape, F32)
         add_sensitivity(STEPS)
         lax.fori_loop(2, STEPS + 1, adjoint, 0)
+        settle()
 
         squash = 1.0 / (1.0 + jnp.exp(-de[OWN]))
         gradient = sens[...] * ma[OWN].astype(F32) * SPAN_EPS * squash * (1.0 - squash)
@@ -464,7 +495,10 @@
             tile = tile + square[8 * i : 8 * (i + 1)]
         factor = RATE / jnp.sqrt(reduce_norm(tile) / cells_total + EPSILON)
         if last:
-            new_out[...] = de[OWN] + factor * gradient
+            new_own[...] = de[OWN] + factor * gradient
+            results.append(pltpu.make_async_copy(new_own, new_out, local_sem.at[1]))
+            results[-1].start()
+            settle()
         else:
             for side in (0, 1):
 
@@ -473,6 +507,7 @@
                     grad_halo(side).wait_recv()
 
             de[...] = de[...] + factor * grads[...]
+            settle()
             for side in (0, 1):
 
                 @pl.when(sends[side])
@@ -486,19 +521,25 @@
             for copy in halo(side):
                 copy.wait_send()
 
-    final.wait()
+    for move in results:
+        move.wait()
 
 
 def body(n, e_start, h_start, background, design, design_mask, plane_counts, plane_rows, source_cells, source_amp, target):
     rows, depth, width = background.shape
     block = rows * depth
     groups = n // GROUP
-    tables = make_tables(width, depth, rows, n)
+    small = [
+        plane_counts.reshape(1, 1),
+        plane_rows,
+        source_cells.reshape(1, -1),
+        source_amp.reshape(1, -1),
+        target,
+        *make_tables(width, depth, rows, n),
+    ]
     far_scale = 1.0 / math.sqrt(width * depth * PLANES_DEV * n * STEPS)
     near_scale = 1.0 / math.sqrt(KY * KZ)
-    vmem = pl.BlockSpec(memory_space=pltpu.VMEM)
-    smem = pl.BlockSpec(memory_space=pltpu.SMEM)
-    hbm = pl.BlockSpec(memory_space=pl.ANY)
+    hbm = pl.BlockSpec(memory_space=pltpu.HBM)
     dma = pltpu.SemaphoreType.DMA
     fields = (3, 3 * block + depth, width)
     new_design, final_field, intensity = pl.pallas_call(
@@ -510,9 +551,10 @@
             jax.ShapeDtypeStruct((3, block, width), F32),
             jax.ShapeDtypeStruct((KZ, KY), F32),
         ),
-        in_specs=[hbm] * 5 + [smem] * 2 + [vmem] * 8 + [smem],
-        out_specs=(vmem, hbm, vmem),
-        scratch_shapes=[
+        in_specs=[hbm] * 13,
+        out_specs=(hbm,) * 3,
+        scratch_shapes=[pltpu.VMEM(a.shape, a.dtype) for a in small]
+        + [
             pltpu.VMEM((STEPS + 1,) + fields, F32),
             pltpu.VMEM((STEPS + 1,) + fields, F32),
             pltpu.VMEM((3 * block, width), F32),
@@ -531,11 +573,11 @@
             pltpu.VMEM((GROUP, KZ // 4, KY), F32),
             pltpu.VMEM((GROUP, KZ // 4, KY), F32),
             pltpu.VMEM((groups, KZ // 4, KY), F32),
-            pltpu.VMEM((KZ // 4, KY), F32),
             pltpu.VMEM((GROUP, 8, width), F32),
             pltpu.VMEM((groups, 8, width), F32),
-            pltpu.VMEM((8, width), F32),
-            dma((5,)),
+            pltpu.VMEM((block, width), F32),
+            pltpu.VMEM((KZ, KY), F32),
+            dma((13,)),
             dma((2, 6)),
             dma((2, 6)),
             dma((2,)),
@@ -544,7 +586,7 @@
         + [dma((GROUP,))] * 6
         + [dma((groups,))] * 4,
         compiler_params=pltpu.CompilerParams(
-            collective_id=0, has_side_effects=True, vmem_limit_bytes=40 * 1024 * 1024
+            collective_id=0, has_side_effects=True, vmem_limit_bytes=64 * 1024 * 1024
         ),
     )(
         e_start.reshape(3, block, width),
@@ -552,12 +594,7 @@
         background.reshape(block, width),
         design.reshape(block, width),
         design_mask.reshape(block, width),
-        plane_counts,
-        plane_rows,
-        source_cells.reshape(1, -1),
-        source_amp.reshape(1, -1),
-        target,
-        *tables,
+        *small,
     )
     return (
         new_design.reshape(rows, depth, width),

time: 88 us -> 74.6 us (0.85)
  local copies, waits for them, and re-layouts: 11 us -> 3.7 us
  Pallas kernels: 75 us -> 69.4 us
    unnamed x33 -> x5, local copies, waits for them, and re-layouts: 11 us -> 3.7 us
    pallas_call x1, Pallas kernels: 75 us -> 69.4 us  [body(): pl.pallas_call(functools.partial(kernel, n, rows, depth, far_scale, near_...]
where the time goes in v2:
time: 74.6 us; the launch traced here: 74.3 us
  Pallas kernels  69.4 us (93%)
  local copies, waits for them, and re-layouts  3.7 us (5%)
  between operations  1.29 us (2%)
    pallas_call x1, Pallas kernels, body(): pl.pallas_call(functools.partial(kernel, n, rows, depth, far_scale, near_...  69.4 us
    unnamed x5, local copies, waits for them, and re-layouts  3.7 us

profile of v2, /device:TPU:0, one launch (start us, length us, event | category | flops | bytes accessed | tf_op | source)
XLA Modules:
  0.0 74.3 jit_solution(12375465358885152031)
XLA Ops:
  1.3 69.4 %shard_map.148 = (f32[128,128]{1,0:T(8,128)}, f32[3,128,128]{2,1,0:T(8,128)}, f32[16,128]{1,0:T(8,128)}) custom-call(f32[3,128,128]{2,1,0:T(8,128)} %bitcast.11, f32[3,128,128]{2,1,0:T(8,128)} %bitcast.12, f32[128,128]{1,0:T(8,128)} %bitcast.14, f32[128,128]{1,0:T(8,128)} %bitcast.15, s32[128,128]{1,0:T(8,128)} %bitcast.16, s32[1,1]{1,0:T(1,128)} %bitcast.10.rest_0_, ...), custom_call_target="tpu_custom_call" | custom-call | tf_op jit(solution)/shard_map/pallas_call | solution.py:545
  70.6 1.5 %copy.20 = f32[8,16,128]{2,1,0:T(8,128)} copy(f32[8,16,128]{2,1,0:T(8,128)} %bitcast.17) | data formatting | bytes 131072
  72.1 0.0 copy-start
  72.1 1.6 %copy.21 = f32[3,8,16,128]{3,2,1,0:T(8,128)} copy(f32[3,8,16,128]{3,2,1,0:T(8,128)} %bitcast.13) | data formatting | bytes 393216
  73.7 0.0 copy-done
  73.7 0.6 copy.22
Async XLA Ops:
  72.1 1.6 %copy-start = (f32[16,128]{1,0:T(8,128)S(1)}, f32[16,128]{1,0:T(8,128)}, u32[]{:S(2)}) copy-start(f32[16,128]{1,0:T(8,128)} %get-tuple-element.14) | copy-start | bytes 24580

commit v3 on v2

--- a/solution.py
+++ b/solution.py
@@ -158,9 +158,18 @@
     hit = jnp.where((at_row == slots[...]) & (at_slot < counts[...]), 1.0, 0.0)
     marks[1] = jnp.broadcast_to(jnp.sum(hit, axis=1, keepdims=True), (rows, width))
 
+    for move in moves[2:]:
+        move.wait()
+
+    def set_inverse(at, inside=None):
+        squash = 1.0 / (1.0 + jnp.exp(-de[at]))
+        scale = COURANT / (bg[at] + SPAN_EPS * ma[at].astype(F32) * squash)
+        inv[at] = scale if inside is None else jnp.where(inside, scale, 0.0)
+
+    set_inverse(OWN)
     pl.semaphore_wait(barrier, greetings)
 
-    def halo(side):
+    def halo(side, early):
         other = device(jnp.clip(me + (1 if side == 0 else -1), 0, n - 1))
         where = ghost[side]
         pairs = [
@@ -170,13 +179,16 @@
             (de_in, de.at[where]),
             (ma_in, ma.at[where]),
             (marks.at[1], marks.at[2 * side]),
+            (inv.at[OWN], inv.at[where]),
         ]
+        taken = (0, 1, 6) if early else (2, 3, 4, 5)
         return [
             pltpu.make_async_remote_copy(
                 src_ref=a, dst_ref=b, send_sem=halo_send.at[side, i], recv_sem=halo_recv.at[side, i],
                 device_id=other, device_id_type=MESH,
             )
             for i, (a, b) in enumerate(pairs)
+            if i in taken
         ]
 
     def grad_halo(side):
@@ -193,7 +205,7 @@
 
         @pl.when(sends[side])
         def _():
-            for copy in halo(side):
+            for copy in halo(side, True):
                 copy.start()
 
         @pl.when(jnp.logical_not(comes[side]))
@@ -201,6 +213,7 @@
             where = ghost[side]
             eh[0, :, where] = jnp.zeros((3, block, width), F32)
             hh[0, :, where] = jnp.zeros((3, block, width), F32)
+            inv[where] = jnp.zeros((block, width), F32)
             bg[where] = jnp.ones((block, width), F32)
             de[where] = jnp.zeros((block, width), F32)
             ma[where] = jnp.zeros((block, width), jnp.int32)
@@ -223,14 +236,21 @@
     phase[0] = base_c * near_c - base_s * near_s
     phase[1] = base_s * near_c + base_c * near_s
 
-    for move in moves:
+    for move in moves[:2]:
         move.wait()
     for side in (0, 1):
 
         @pl.when(comes[side])
         def _():
-            for copy in halo(side):
+            for copy in halo(side, True):
                 copy.wait_recv()
+
+    for side in (0, 1):
+
+        @pl.when(sends[side])
+        def _():
+            for copy in halo(side, False):
+                copy.start()
 
     span = CH * depth
     y_at = lax.broadcasted_iota(jnp.int32, (span, width), 1)
@@ -396,13 +416,10 @@
     results = []
     for iteration in range(ITERS):
         last = iteration == ITERS - 1
-        for c in range(3):
-            at = pl.ds(c * block, block)
-            squash = 1.0 / (1.0 + jnp.exp(-de[at]))
-            scale = COURANT / (bg[at] + SPAN_EPS * ma[at].astype(F32) * squash)
-            if c != 1:
-                scale = jnp.where(comes[0] if c == 0 else comes[1], scale, 0.0)
-            inv[at] = scale
+        if iteration > 0:
+            set_inverse(ghost[0], comes[0])
+            set_inverse(OWN)
+            set_inverse(ghost[1], comes[1])
         lax.fori_loop(1, STEPS + 1, forward, 0)
         if last:
             results.append(pltpu.make_async_copy(eh.at[STEPS, :, OWN], final_out, local_sem.at[0]))
@@ -440,6 +457,18 @@
             for i in range(8):
                 part[8 * f + i] = far[lines * i : lines * (i + 1)]
         reduce_far()
+        if iteration == 0:
+            for side in (0, 1):
+
+                @pl.when(comes[side])
+                def _():
+                    for copy in halo(side, False):
+                        copy.wait_recv()
+
+                @pl.when(sends[side])
+                def _():
+                    for copy in halo(side, True) + halo(side, False):
+                        copy.wait_send()
 
         power = jnp.zeros((KZ, KY), F32)
         for f in (0, 1):
@@ -513,13 +542,6 @@
                 @pl.when(sends[side])
                 def _():
                     grad_halo(side).wait_send()
-
-    for side in (0, 1):
-
-        @pl.when(sends[side])
-        def _():
-            for copy in halo(side):
-                copy.wait_send()
 
     for move in results:
         move.wait()
@@ -578,8 +600,8 @@
             pltpu.VMEM((block, width), F32),
             pltpu.VMEM((KZ, KY), F32),
             dma((13,)),
-            dma((2, 6)),
-            dma((2, 6)),
+            dma((2, 7)),
+            dma((2, 7)),
             dma((2,)),
             dma((2,)),
         ]

time: 74.6 us -> 73.7 us (0.988)
  Pallas kernels: 69.4 us -> 68.5 us
    pallas_call x1, Pallas kernels: 69.4 us -> 68.5 us  [body(): pl.pallas_call(functools.partial(kernel, n, rows, depth, far_scale, near_...]
where the time goes in v3:
time: 73.7 us; the launch traced here: 73.5 us
  Pallas kernels  68.5 us (93%)
  local copies, waits for them, and re-layouts  3.7 us (5%)
  between operations  1.29 us (2%)
    pallas_call x1, Pallas kernels, body(): pl.pallas_call(functools.partial(kernel, n, rows, depth, far_scale, near_...  68.5 us
    unnamed x5, local copies, waits for them, and re-layouts  3.7 us

profile of v3, /device:TPU:0, one launch (start us, length us, event | category | flops | bytes accessed | tf_op | source)
XLA Modules:
  0.0 73.5 jit_solution(13793248462457815087)
XLA Ops:
  1.3 68.5 %shard_map.148 = (f32[128,128]{1,0:T(8,128)}, f32[3,128,128]{2,1,0:T(8,128)}, f32[16,128]{1,0:T(8,128)}) custom-call(f32[3,128,128]{2,1,0:T(8,128)} %bitcast.11, f32[3,128,128]{2,1,0:T(8,128)} %bitcast.12, f32[128,128]{1,0:T(8,128)} %bitcast.14, f32[128,128]{1,0:T(8,128)} %bitcast.15, s32[128,128]{1,0:T(8,128)} %bitcast.16, s32[1,1]{1,0:T(1,128)} %bitcast.10.rest_0_, ...), custom_call_target="tpu_custom_call" | custom-call | tf_op jit(solution)/shard_map/pallas_call | solution.py:567
  69.8 1.5 %copy.20 = f32[8,16,128]{2,1,0:T(8,128)} copy(f32[8,16,128]{2,1,0:T(8,128)} %bitcast.17) | data formatting | bytes 131072
  71.3 0.0 copy-start
  71.3 1.6 %copy.21 = f32[3,8,16,128]{3,2,1,0:T(8,128)} copy(f32[3,8,16,128]{3,2,1,0:T(8,128)} %bitcast.13) | data formatting | bytes 393216
  72.9 0.0 copy-done
  72.9 0.6 copy.22
Async XLA Ops:
  71.3 1.6 %copy-start = (f32[16,128]{1,0:T(8,128)S(1)}, f32[16,128]{1,0:T(8,128)}, u32[]{:S(2)}) copy-start(f32[16,128]{1,0:T(8,128)} %get-tuple-element.14) | copy-start | bytes 24580
